TPU v7x, 32 devices: a whole 2x2x4 slice. The times are simulated.
32 devices in a mesh: groups: 2 (over x), ctx: 16 (over z, y, core).
Axes of the slice: x: 2, y: 2, z: 4, core: 2. Of those that a mesh axis runs over, the one named last changes fastest.
Arguments:
- queries: bfloat16 [6144, 2048], P(('groups', 'ctx')), parts along dimension 0, may hold values from -6 to 6
- patch_keys: bfloat16 [6144, 512], P(('groups', 'ctx')), parts along dimension 0, may hold values from -6 to 6
- patch_values: bfloat16 [6144, 512], P(('groups', 'ctx')), parts along dimension 0, may hold values from -6 to 6
- patch_counts: int32 [32], P('groups'), parts along dimension 0, may hold values from 64 to 192, as said below
Outputs:
- attended: bfloat16 [6144, 2048], P(('groups', 'ctx')), parts along dimension 0
There are 2 independent parts, one for each index of `groups`. A program takes and returns all parts, laid end to end along the dimension named above; each array names one. Nothing has to cross between parts.
Inputs may be any that keep to these rules, and one draw needn't show every extreme that they name: patch_counts[i] patches fill slots 0 to patch_counts[i] - 1 of shard i; the counts sum to 2048, and starts[i] differs from i * 128 by at most a quarter of 128.
All inputs are finite; a program needn't handle non-finite values.
Results may differ from a plain program's by a relative error of at most 0.0044.
Values may be sent and summed in bfloat16 or wider, within the bound.
A program may use at most 192 MiB of HBM per device.

v0:
```python
import jax
import jax.numpy as jnp
from jax import lax
from jax.sharding import PartitionSpec as P

Q_HEADS = 16
KV_HEADS = 4
HEAD_DIM = 128
GROUP = 4


masked_score = -1e30
far_place = 2**30


def block_count(length):
    pieces = max(1, length // 512)
    while length % pieces:
        pieces -= 1
    return pieces


def attend(query_rows, query_place, key_rows, value_rows, key_place, key_live):
    row_total = query_rows.shape[0]
    length = key_rows.shape[0]
    pieces = block_count(length)
    block_len = length // pieces
    grouped = query_rows.reshape(row_total, KV_HEADS, GROUP, HEAD_DIM)
    key_blocks = key_rows.reshape(pieces, block_len, KV_HEADS, HEAD_DIM)
    value_blocks = value_rows.reshape(pieces, block_len, KV_HEADS, HEAD_DIM)
    place_blocks = key_place.reshape(pieces, block_len)
    live_blocks = key_live.reshape(pieces, block_len)
    block_lowest = jnp.min(jnp.where(live_blocks, place_blocks, far_place), axis=1)
    needed = block_lowest <= jnp.max(query_place)
    score_scale = HEAD_DIM ** (-0.5)

    def accumulate(running, blocks):
        key_block, value_block, place_block, live_block, block_needed = blocks

        def compute(current):
            running_max, weight_sum, blended = current
            direct = (
                jnp.einsum("rkgd,mkd->kgrm", grouped, key_block, preferred_element_type=jnp.float32)
                * score_scale
            )
            visible = live_block[None, :] & (place_block[None, :] <= query_place[:, None])
            scores = jnp.where(visible, direct, masked_score)
            new_max = jnp.maximum(running_max, jnp.max(scores, axis=-1))
            rescale = jnp.exp(running_max - new_max)
            weights = jnp.exp(scores - new_max[..., None])
            weight_sum = weight_sum * rescale + jnp.sum(weights, axis=-1)
            rounded = weights.astype(jnp.bfloat16)
            blended = blended * rescale[..., None] + jnp.einsum(
                "kgrm,mkd->kgrd", rounded, value_block, preferred_element_type=jnp.float32
            )
            return (new_max, weight_sum, blended)

        return (lax.cond(block_needed, compute, lambda current: current, running), None)

    initial = (
        jnp.full((KV_HEADS, GROUP, row_total), masked_score, jnp.float32),
        jnp.zeros((KV_HEADS, GROUP, row_total), jnp.float32),
        jnp.zeros((KV_HEADS, GROUP, row_total, HEAD_DIM), jnp.float32),
    )
    (_, weight_sum, blended), _ = lax.scan(
        accumulate, initial, (key_blocks, value_blocks, place_blocks, live_blocks, needed)
    )
    blended = blended / weight_sum[..., None]
    return blended.transpose(2, 0, 1, 3).reshape(row_total, Q_HEADS * HEAD_DIM)


def per_device(queries, patch_keys, patch_values, patch_counts):
    slot_total = queries.shape[0]
    device_rank = lax.axis_index("ctx")
    starts = jnp.cumsum(patch_counts) - patch_counts
    own_start = starts[device_rank]
    own_count = patch_counts[device_rank]
    slot_order = jnp.arange(slot_total, dtype=jnp.int32)
    own_place = own_start + slot_order
    own_live = slot_order < own_count
    key_all, value_all = (
        lax.all_gather(patch_keys, "ctx", axis=0, tiled=True),
        lax.all_gather(patch_values, "ctx", axis=0, tiled=True),
    )
    key_place = (starts[:, None] + slot_order[None, :]).reshape(-1)
    key_live = (slot_order[None, :] < patch_counts[:, None]).reshape(-1)
    result = attend(queries, own_place, key_all, value_all, key_place, key_live)
    return jnp.where(own_live[:, None], result, 0.0).astype(jnp.bfloat16)


def solution(mesh):
    placed = (
        P(("groups", "ctx"), None),
        P(("groups", "ctx"), None),
        P(("groups", "ctx"), None),
        P("groups"),
    )
    return jax.shard_map(
        per_device,
        mesh=mesh,
        in_specs=placed,
        out_specs=P(("groups", "ctx"), None),
        check_vma=False,
    )
```

profile of v0, /device:TPU:25, one launch (start us, length us, event | category | flops | bytes accessed | tf_op | source)
XLA Modules:
  0.0 180.7 jit_solution(18061164444423349356)
XLA Ops:
  13.7 2.3 %reshape.61 = bf16[192,4,4,128]{3,2,1,0:T(4,128)(2,1)S(1)} reshape(bf16[192,2048]{1,0:T(8,128)(2,1)} %param.8) | data formatting | bytes 1572864 | tf_op jit(solution)/shard_map/reshape | solution.py:28
  17.6 37.6 %all-gather.3.cloned.1.call-done = bf16[3072,512]{1,0:T(8,128)(2,1)} async-done(((bf16[192,512]{1,0:T(8,128)(2,1)}), bf16[3072,512]{1,0:T(8,128)(2,1)}) %all-gather.3.cloned.1.call-update) | async-done | bytes 3145744 | tf_op jit(solution)/shard_map/all_gather | solution.py:82
  55.1 5.6 %reshape.60 = bf16[6,512,4,128]{3,2,1,0:T(4,128)(2,1)} reshape(bf16[3072,512]{1,0:T(8,128)(2,1)} %all-gather.3.cloned.1.call-done) | data formatting | bytes 6291456 | tf_op jit(solution)/shard_map/reshape | solution.py:29
  60.7 4.2 %copy.13 = bf16[6,512,4,128]{3,1,2,0:T(8,128)(2,1)} copy(bf16[6,512,4,128]{3,2,1,0:T(4,128)(2,1)} %reshape.60) | data formatting | bytes 6291456
  64.9 36.5 %all-gather.5.cloned.1.call-done = bf16[3072,512]{1,0:T(8,128)(2,1)} async-done(((bf16[192,512]{1,0:T(8,128)(2,1)}), bf16[3072,512]{1,0:T(8,128)(2,1)}) %all-gather.5.cloned.1.call-update) | async-done | bytes 3145744 | tf_op jit(solution)/shard_map/all_gather | solution.py:83
  101.5 5.6 %reshape.62 = bf16[6,512,4,128]{3,2,1,0:T(4,128)(2,1)} reshape(bf16[3072,512]{1,0:T(8,128)(2,1)} %all-gather.5.cloned.1.call-done) | data formatting | bytes 6291456 | tf_op jit(solution)/shard_map/reshape | solution.py:30
  107.0 4.3 %copy.15 = bf16[6,512,4,128]{3,1,2,0:T(8,128)(2,1)} copy(bf16[6,512,4,128]{3,2,1,0:T(4,128)(2,1)} %reshape.62) | data formatting | bytes 6291456
  111.5 59.5 %while.15 = (s32[]{:T(128)}, f32[4,4,192]{2,1,0:T(4,128)S(1)}, f32[4,4,192]{2,1,0:T(4,128)S(1)}, f32[4,4,192,128]{3,2,1,0:T(8,128)S(1)}, pred[6]{0:T(512)(128)(4...) while((s32[]{:T(128)}, f32[4,4,192]{2,1,0:T(4,128)S(1)}, ...), condition=%wide.region_8.9_spmd.clone, body=%wide.region_3.8_spmd.clone.sunk | while | flops 823603392 | bytes 24540076 | solution.py:65
  112.7 8.7 %conditional.3 = ((f32[4,4,192]{2,1,0:T(4,128)S(1)}, f32[4,4,192]{2,1,0:T(4,128)S(1)}, f32[4,4,192,128]{3,2,1,0:T(8,128)S(1)})) conditional(s32[]{:T(128)} %bitcast.40, (f32[4,4,192]{2,1,0:T(4,128)S(1)}, f32[4,4,192]{2,1,0:T(4,128)S(1)}, f32[4,4,192,128]{3,2,1,0:T(8,128)S(1)}) %tuple.41, (s32[16,192]{1,0:T(8,128)S(1)}, s32[]{:T(128)}, ...), branch_computations={%region_4.4_spmd, %region_5.7_spmd} | conditional | flops 823603392 | bytes 24526764 | solution.py:58
  113.9 2.2 %fusion.8 = (f32[4,4,192]{2,1,0:T(4,128)S(1)}, f32[4,512,192,4]{1,2,3,0:T(8,128)S(1)}) fusion(pred[192,512]{1,0:T(8,128)(4,1)S(1)} %compare_and_fusion, bf16[192,4,4,128]{3,0,2,1:T(8,128)(2,1)S(1)} %get-tuple-element.144, bf16[6,512,4,128]{3,1,2,0:T(8,128)(2,1)} %get-tuple-element.143, s32[]{:T(128)} %get-tuple-element.140), kind=kOutput, calls=%fused_computation.7 | convolution fusion | flops 407368704 | bytes 7713280 | tf_op jit(solution)/shard_map/while/body/eval_jaxpr/cond/branch_1_fun/rkgd,mkd->kgrm/dot_general | solution.py:43
  118.1 3.3 %multiply_add_fusion = f32[4,4,192,128]{3,2,1,0:T(8,128)S(1)} fusion(f32[4,4,192,128]{3,2,1,0:T(8,128)S(1)} %get-tuple-element.146, f32[4,512,192,4]{1,2,3,0:T(8,128)S(1)} %get-tuple-element.257, f32[4,4,192]{2,1,0:T(4,128)S(1)} %max.4, pred[192,512]{1,0:T(8,128)(4,1)S(1)} %compare_and_fusion, f32[4,4,192]{2,1,0:T(4,128)S(1)} %bitcast.46, ...), kind=kOutput, calls=%fused_computation.13 | convolution fusion | flops 409731072 | bytes 10084864 | tf_op jit(solution)/shard_map/while/body/eval_jaxpr/cond/branch_1_fun/kgrm,mkd->kgrd/dot_general | solution.py:53
  122.6 8.7 %conditional.3 = ((f32[4,4,192]{2,1,0:T(4,128)S(1)}, f32[4,4,192]{2,1,0:T(4,128)S(1)}, f32[4,4,192,128]{3,2,1,0:T(8,128)S(1)})) conditional(s32[]{:T(128)} %bitcast.40, (f32[4,4,192]{2,1,0:T(4,128)S(1)}, f32[4,4,192]{2,1,0:T(4,128)S(1)}, f32[4,4,192,128]{3,2,1,0:T(8,128)S(1)}) %tuple.41, (s32[16,192]{1,0:T(8,128)S(1)}, s32[]{:T(128)}, ...), branch_computations={%region_4.4_spmd, %region_5.7_spmd} | conditional | flops 823603392 | bytes 24526764 | solution.py:58
  123.8 2.2 %fusion.8 = (f32[4,4,192]{2,1,0:T(4,128)S(1)}, f32[4,512,192,4]{1,2,3,0:T(8,128)S(1)}) fusion(pred[192,512]{1,0:T(8,128)(4,1)S(1)} %compare_and_fusion, bf16[192,4,4,128]{3,0,2,1:T(8,128)(2,1)S(1)} %get-tuple-element.144, bf16[6,512,4,128]{3,1,2,0:T(8,128)(2,1)} %get-tuple-element.143, s32[]{:T(128)} %get-tuple-element.140), kind=kOutput, calls=%fused_computation.7 | convolution fusion | flops 407368704 | bytes 7713280 | tf_op jit(solution)/shard_map/while/body/eval_jaxpr/cond/branch_1_fun/rkgd,mkd->kgrm/dot_general | solution.py:43
  128.0 3.3 %multiply_add_fusion = f32[4,4,192,128]{3,2,1,0:T(8,128)S(1)} fusion(f32[4,4,192,128]{3,2,1,0:T(8,128)S(1)} %get-tuple-element.146, f32[4,512,192,4]{1,2,3,0:T(8,128)S(1)} %get-tuple-element.257, f32[4,4,192]{2,1,0:T(4,128)S(1)} %max.4, pred[192,512]{1,0:T(8,128)(4,1)S(1)} %compare_and_fusion, f32[4,4,192]{2,1,0:T(4,128)S(1)} %bitcast.46, ...), kind=kOutput, calls=%fused_computation.13 | convolution fusion | flops 409731072 | bytes 10084864 | tf_op jit(solution)/shard_map/while/body/eval_jaxpr/cond/branch_1_fun/kgrm,mkd->kgrd/dot_general | solution.py:53
  132.5 8.7 %conditional.3 = ((f32[4,4,192]{2,1,0:T(4,128)S(1)}, f32[4,4,192]{2,1,0:T(4,128)S(1)}, f32[4,4,192,128]{3,2,1,0:T(8,128)S(1)})) conditional(s32[]{:T(128)} %bitcast.40, (f32[4,4,192]{2,1,0:T(4,128)S(1)}, f32[4,4,192]{2,1,0:T(4,128)S(1)}, f32[4,4,192,128]{3,2,1,0:T(8,128)S(1)}) %tuple.41, (s32[16,192]{1,0:T(8,128)S(1)}, s32[]{:T(128)}, ...), branch_computations={%region_4.4_spmd, %region_5.7_spmd} | conditional | flops 823603392 | bytes 24526764 | solution.py:58
  137.9 3.3 %multiply_add_fusion = f32[4,4,192,128]{3,2,1,0:T(8,128)S(1)} fusion(f32[4,4,192,128]{3,2,1,0:T(8,128)S(1)} %get-tuple-element.146, f32[4,512,192,4]{1,2,3,0:T(8,128)S(1)} %get-tuple-element.257, f32[4,4,192]{2,1,0:T(4,128)S(1)} %max.4, pred[192,512]{1,0:T(8,128)(4,1)S(1)} %compare_and_fusion, f32[4,4,192]{2,1,0:T(4,128)S(1)} %bitcast.46, ...), kind=kOutput, calls=%fused_computation.13 | convolution fusion | flops 409731072 | bytes 10084864 | tf_op jit(solution)/shard_map/while/body/eval_jaxpr/cond/branch_1_fun/kgrm,mkd->kgrd/dot_general | solution.py:53
  142.5 8.7 %conditional.3 = ((f32[4,4,192]{2,1,0:T(4,128)S(1)}, f32[4,4,192]{2,1,0:T(4,128)S(1)}, f32[4,4,192,128]{3,2,1,0:T(8,128)S(1)})) conditional(s32[]{:T(128)} %bitcast.40, (f32[4,4,192]{2,1,0:T(4,128)S(1)}, f32[4,4,192]{2,1,0:T(4,128)S(1)}, f32[4,4,192,128]{3,2,1,0:T(8,128)S(1)}) %tuple.41, (s32[16,192]{1,0:T(8,128)S(1)}, s32[]{:T(128)}, ...), branch_computations={%region_4.4_spmd, %region_5.7_spmd} | conditional | flops 823603392 | bytes 24526764 | solution.py:58
  147.8 3.3 %multiply_add_fusion = f32[4,4,192,128]{3,2,1,0:T(8,128)S(1)} fusion(f32[4,4,192,128]{3,2,1,0:T(8,128)S(1)} %get-tuple-element.146, f32[4,512,192,4]{1,2,3,0:T(8,128)S(1)} %get-tuple-element.257, f32[4,4,192]{2,1,0:T(4,128)S(1)} %max.4, pred[192,512]{1,0:T(8,128)(4,1)S(1)} %compare_and_fusion, f32[4,4,192]{2,1,0:T(4,128)S(1)} %bitcast.46, ...), kind=kOutput, calls=%fused_computation.13 | convolution fusion | flops 409731072 | bytes 10084864 | tf_op jit(solution)/shard_map/while/body/eval_jaxpr/cond/branch_1_fun/kgrm,mkd->kgrd/dot_general | solution.py:53
  152.4 8.7 %conditional.3 = ((f32[4,4,192]{2,1,0:T(4,128)S(1)}, f32[4,4,192]{2,1,0:T(4,128)S(1)}, f32[4,4,192,128]{3,2,1,0:T(8,128)S(1)})) conditional(s32[]{:T(128)} %bitcast.40, (f32[4,4,192]{2,1,0:T(4,128)S(1)}, f32[4,4,192]{2,1,0:T(4,128)S(1)}, f32[4,4,192,128]{3,2,1,0:T(8,128)S(1)}) %tuple.41, (s32[16,192]{1,0:T(8,128)S(1)}, s32[]{:T(128)}, ...), branch_computations={%region_4.4_spmd, %region_5.7_spmd} | conditional | flops 823603392 | bytes 24526764 | solution.py:58
  153.5 2.2 %fusion.8 = (f32[4,4,192]{2,1,0:T(4,128)S(1)}, f32[4,512,192,4]{1,2,3,0:T(8,128)S(1)}) fusion(pred[192,512]{1,0:T(8,128)(4,1)S(1)} %compare_and_fusion, bf16[192,4,4,128]{3,0,2,1:T(8,128)(2,1)S(1)} %get-tuple-element.144, bf16[6,512,4,128]{3,1,2,0:T(8,128)(2,1)} %get-tuple-element.143, s32[]{:T(128)} %get-tuple-element.140), kind=kOutput, calls=%fused_computation.7 | convolution fusion | flops 407368704 | bytes 7713280 | tf_op jit(solution)/shard_map/while/body/eval_jaxpr/cond/branch_1_fun/rkgd,mkd->kgrm/dot_general | solution.py:43
  157.8 3.3 %multiply_add_fusion = f32[4,4,192,128]{3,2,1,0:T(8,128)S(1)} fusion(f32[4,4,192,128]{3,2,1,0:T(8,128)S(1)} %get-tuple-element.146, f32[4,512,192,4]{1,2,3,0:T(8,128)S(1)} %get-tuple-element.257, f32[4,4,192]{2,1,0:T(4,128)S(1)} %max.4, pred[192,512]{1,0:T(8,128)(4,1)S(1)} %compare_and_fusion, f32[4,4,192]{2,1,0:T(4,128)S(1)} %bitcast.46, ...), kind=kOutput, calls=%fused_computation.13 | convolution fusion | flops 409731072 | bytes 10084864 | tf_op jit(solution)/shard_map/while/body/eval_jaxpr/cond/branch_1_fun/kgrm,mkd->kgrd/dot_general | solution.py:53
  162.3 8.7 %conditional.3 = ((f32[4,4,192]{2,1,0:T(4,128)S(1)}, f32[4,4,192]{2,1,0:T(4,128)S(1)}, f32[4,4,192,128]{3,2,1,0:T(8,128)S(1)})) conditional(s32[]{:T(128)} %bitcast.40, (f32[4,4,192]{2,1,0:T(4,128)S(1)}, f32[4,4,192]{2,1,0:T(4,128)S(1)}, f32[4,4,192,128]{3,2,1,0:T(8,128)S(1)}) %tuple.41, (s32[16,192]{1,0:T(8,128)S(1)}, s32[]{:T(128)}, ...), branch_computations={%region_4.4_spmd, %region_5.7_spmd} | conditional | flops 823603392 | bytes 24526764 | solution.py:58
  163.5 2.2 %fusion.8 = (f32[4,4,192]{2,1,0:T(4,128)S(1)}, f32[4,512,192,4]{1,2,3,0:T(8,128)S(1)}) fusion(pred[192,512]{1,0:T(8,128)(4,1)S(1)} %compare_and_fusion, bf16[192,4,4,128]{3,0,2,1:T(8,128)(2,1)S(1)} %get-tuple-element.144, bf16[6,512,4,128]{3,1,2,0:T(8,128)(2,1)} %get-tuple-element.143, s32[]{:T(128)} %get-tuple-element.140), kind=kOutput, calls=%fused_computation.7 | convolution fusion | flops 407368704 | bytes 7713280 | tf_op jit(solution)/shard_map/while/body/eval_jaxpr/cond/branch_1_fun/rkgd,mkd->kgrm/dot_general | solution.py:43
  167.7 3.3 %multiply_add_fusion = f32[4,4,192,128]{3,2,1,0:T(8,128)S(1)} fusion(f32[4,4,192,128]{3,2,1,0:T(8,128)S(1)} %get-tuple-element.146, f32[4,512,192,4]{1,2,3,0:T(8,128)S(1)} %get-tuple-element.257, f32[4,4,192]{2,1,0:T(4,128)S(1)} %max.4, pred[192,512]{1,0:T(8,128)(4,1)S(1)} %compare_and_fusion, f32[4,4,192]{2,1,0:T(4,128)S(1)} %bitcast.46, ...), kind=kOutput, calls=%fused_computation.13 | convolution fusion | flops 409731072 | bytes 10084864 | tf_op jit(solution)/shard_map/while/body/eval_jaxpr/cond/branch_1_fun/kgrm,mkd->kgrd/dot_general | solution.py:53
  (120 shorter events, 38.2 us)
Async XLA Ops:
  6.5 48.6 %all-gather.3.cloned.1.call-start = ((), (), s32[]{:S(2)}) async-start(), calls=%async_computation | async-start | bytes 3342336 | tf_op jit(solution)/shard_map/all_gather | solution.py:82
  7.3 94.2 %all-gather.5.cloned.1.call-start = ((), (), s32[]{:S(2)}) async-start(), calls=%async_computation.1 | async-start | bytes 3342336 | tf_op jit(solution)/shard_map/all_gather | solution.py:83
  107.0 4.5 %copy-start = (s32[16]{0:T(128)S(1)}, s32[16]{0:T(128)}, u32[]{:S(2)}) copy-start(s32[16]{0:T(128)} %param.11) | copy-start | bytes 196
Sparse Core Ops, SparseCore 0:
  9.6 45.4 all-gather.2
  57.4 43.9 all-gather.4
where the time goes:
time: 182 us; the launch traced here: 181 us
  waiting for transfers between devices  75.5 us (41%)
  matrix products  33.3 us (18%)
  local copies, waits for them, and re-layouts  31.1 us (17%)
  other arithmetic  23.1 us (13%)
  between operations  13.5 us (7%)
  loops' own time  4.08 us (2%)
    all_gather x1, waiting for transfers between devices, per_device(): lax.all_gather(patch_keys, 'ctx', axis=0, tiled=True)  37.6 us
    all_gather x1, waiting for transfers between devices, per_device(): lax.all_gather(patch_values, 'ctx', axis=0, tiled=True)  36.5 us
    dot_general x6, matrix products, compute(): jnp.einsum('kgrm,mkd->kgrd', rounded, value_block, preferred_element_type...  19.9 us
    dot_general x6, matrix products, compute(): jnp.einsum('rkgd,mkd->kgrm', grouped, key_block, preferred_element_type=j...  13.4 us
    reduce_sum x6, other arithmetic, compute(): weight_sum = weight_sum * rescale + jnp.sum(weights, axis=-1)  11.7 us
    unnamed x5, local copies, waits for them, and re-layouts  8.71 us
    reshape x1, local copies, waits for them, and re-layouts, attend(): value_blocks = value_rows.reshape(pieces, block_len, KV_HEADS, HEAD_DIM)  5.56 us
    reshape x1, local copies, waits for them, and re-layouts, attend(): key_blocks = key_rows.reshape(pieces, block_len, KV_HEADS, HEAD_DIM)  5.56 us
  transfers between devices with their start and end apart: 2, of which 2 were waited for; matrix products, arithmetic and copies ran while one was open for 11% of the time, Pallas kernels for 0%

commit v1 on v0

v1 whole, which is shorter than its diff:
```python
import functools

import jax
import jax.numpy as jnp
from jax import lax
from jax.experimental import pallas as pl
from jax.experimental.pallas import tpu as pltpu
from jax.sharding import PartitionSpec as P

KV_HEADS = 4
GROUP = 4
HEAD_DIM = 128
HIDDEN = -1e30
LOG2E = 1.4426950408889634
EXPONENT_SCALE = LOG2E * HEAD_DIM ** (-0.5)
MESH = pl.DeviceIdType.MESH

FAR_PLACE = 2**20


def kernel(
    ranks,
    q_ref,
    k_ref,
    v_ref,
    counts_ref,
    out_ref,
    near,
    far,
    beside,
    mine,
    edge_out,
    edge_in,
    stacked,
    total,
    highest,
    weight_sum,
    own_send,
    near_send,
    far_send,
    beside_recv,
    near_recv,
    far_recv,
    edge_send,
    edge_recv,
):
    slots = q_ref.shape[0]
    mean = mine.shape[1]
    quarter = edge_in.shape[2]
    planes = ranks // 4
    part_index = lax.axis_index("groups")
    rank = lax.axis_index("ctx")
    plane, row, side = rank // 4, (rank // 2) % 2, rank % 2
    mate = rank + 1 - 2 * side
    over = rank + 2 - 4 * row

    partners = (
        (mate, None),
        (over, None),
        (rank - 1, (side == 0) & (rank > 0)),
        (rank + 1, (side == 1) & (rank < ranks - 1)),
        (rank - 4, plane > 0),
        (rank + 4, plane < planes - 1),
    )
    barrier = pltpu.get_barrier_semaphore()
    expected = 0
    for partner, there in partners:
        if there is None:
            pl.semaphore_signal(barrier, inc=1, device_id=(part_index, partner), device_id_type=MESH)
            expected = expected + 1
        else:

            @pl.when(there)
            def _(partner=partner):
                pl.semaphore_signal(barrier, inc=1, device_id=(part_index, partner), device_id_type=MESH)

            expected = expected + there.astype(jnp.int32)

    own_start = lax.fori_loop(
        0, ranks, lambda j, s: s + jnp.where(j < rank, counts_ref[j], 0), jnp.int32(0)
    )
    own_count = counts_ref[rank]

    place = lax.broadcasted_iota(jnp.int32, (slots, slots), 0) + (mean * rank - quarter - own_start)
    slot = lax.broadcasted_iota(jnp.int32, (slots, slots), 1)
    pick = jnp.where((place == slot) & (slot < own_count), 1.0, 0.0).astype(jnp.bfloat16)
    for part, ref in enumerate((k_ref, v_ref)):
        placed = jnp.dot(pick, ref[...], preferred_element_type=jnp.float32).astype(jnp.bfloat16)
        half = slice(part * HEAD_DIM, (part + 1) * HEAD_DIM)
        for head in range(KV_HEADS):
            rows = placed[:, head * HEAD_DIM : (head + 1) * HEAD_DIM]
            edge_out[0, head, :, half] = rows[:quarter]
            mine[head, :, half] = rows[quarter : quarter + mean]
            edge_out[1, head, :, half] = rows[quarter + mean :]

    pl.semaphore_wait(barrier, expected)

    def edge(which):
        return pltpu.make_async_remote_copy(
            src_ref=edge_out.at[which],
            dst_ref=edge_in.at[which],
            send_sem=edge_send.at[which],
            recv_sem=edge_recv.at[which],
            device_id=(part_index, (rank + 2 * which - 1 + ranks) % ranks),
            device_id_type=MESH,
        )

    first, last = rank == 0, rank == ranks - 1

    @pl.when(jnp.logical_not(first))
    def _():
        edge(0).start()

    @pl.when(jnp.logical_not(last))
    def _():
        edge(1).start()

    def head_columns(head):
        return pl.ds(pl.multiple_of(head * HEAD_DIM, HEAD_DIM), HEAD_DIM)

    def scores_of(keys, head):
        return lax.dot_general(
            keys, stacked[head], (((1,), (1,)), ((), ())), preferred_element_type=jnp.float32
        )

    def blend(values, weights):
        return lax.dot_general(
            values,
            weights.astype(jnp.bfloat16),
            (((0,), (0,)), ((), ())),
            preferred_element_type=jnp.float32,
        )

    lanes = GROUP * slots

    def own(head, _):
        for g in range(GROUP):
            column = pl.multiple_of((head * GROUP + g) * HEAD_DIM, HEAD_DIM)
            stacked[head, g * slots : (g + 1) * slots, :] = q_ref[:, pl.ds(column, HEAD_DIM)]
        scores = scores_of(k_ref[:, head_columns(head)], head)
        key_slot = lax.broadcasted_iota(jnp.int32, (slots, lanes), 0)
        query_slot = lax.broadcasted_iota(jnp.int32, (slots, lanes), 1) % slots
        scores = jnp.where(key_slot <= query_slot, scores, HIDDEN)
        top = jnp.max(scores, axis=0, keepdims=True)
        weights = jnp.exp2((scores - top) * EXPONENT_SCALE)
        highest[head] = top
        weight_sum[head] = jnp.sum(weights, axis=0, keepdims=True)
        total[head] = blend(v_ref[:, head_columns(head)], weights)
        return 0

    lax.fori_loop(0, KV_HEADS, own, 0)

    def absorb(head, rows, visible):
        scores = scores_of(rows[:, :HEAD_DIM], head)
        if visible is not None:
            scores = jnp.where(visible, scores, HIDDEN)
        before = highest[head]
        top = jnp.maximum(before, jnp.max(scores, axis=0, keepdims=True))
        rescale = jnp.exp2((before - top) * EXPONENT_SCALE)
        weights = jnp.exp2((scores - top) * EXPONENT_SCALE)
        highest[head] = top
        weight_sum[head] = weight_sum[head] * rescale + jnp.sum(weights, axis=0, keepdims=True)
        total[head] = total[head] * rescale + blend(rows[:, HEAD_DIM:], weights)

    def before_own(first_place, count):
        return lax.broadcasted_iota(jnp.int32, (count, lanes), 0) + first_place < own_start

    def absorb_pair(pair, mask):
        def one(head, _):
            rows = jnp.concatenate([pair[0, head], pair[1, head]])
            visible = None
            if mask is not None:
                visible = jnp.concatenate(
                    [
                        jnp.full((mean, lanes), True),
                        before_own(jnp.where(mask, mean * (rank - 1), -FAR_PLACE), mean),
                    ]
                )
            absorb(head, rows, visible)
            return 0

        lax.fori_loop(0, KV_HEADS, one, 0)

    def copy(source, landing, send_sem, recv_sem, target):
        return pltpu.make_async_remote_copy(
            src_ref=source,
            dst_ref=landing,
            send_sem=send_sem,
            recv_sem=recv_sem,
            device_id=(part_index, target),
            device_id_type=MESH,
        )

    more = plane < planes - 1

    def own_copies():
        return (
            (row == 0, copy(mine, far[0].at[0], own_send.at[1], far_recv.at[0, 0], over)),
            (more, copy(mine, near[0].at[0], own_send.at[0], near_recv.at[0, 0], rank + 4))
            if planes > 1
            else (None, None),
            (side == 0, copy(mine, beside, own_send.at[2], beside_recv, mate)),
        )

    def near_copies(s):
        here = near[s].at[0]
        along = (None, None)
        if s + 1 < planes - 1:
            landing = near[s + 1].at[0]
            along = (
                more,
                copy(here, landing, near_send.at[s, 0], near_recv.at[s + 1, 0], rank + 4),
            )
        return (
            along,
            (True, copy(here, far[s + 1].at[0], near_send.at[s, 1], far_recv.at[s + 1, 0], over)),
            (True, copy(here, near[s].at[1], near_send.at[s, 2], near_recv.at[s, 1], mate)),
        )

    def far_copies(s):
        return (
            (True, copy(far[s].at[0], far[s].at[1], far_send.at[s], far_recv.at[s, 1], mate)),
        )

    def each(copies, act):
        for wanted, item in copies:
            if wanted is True:
                act(item)
            elif wanted is not None:

                @pl.when(wanted)
                def _(item=item):
                    act(item)

    def start(item):
        item.start()

    def finish(item):
        item.wait_send()

    def arrived(landing, recv_sem):
        copy(landing, landing, own_send.at[0], recv_sem, mate).wait_recv()

    @pl.when(jnp.logical_not(first))
    def _():
        edge(1).wait_recv()
        mine[:, :quarter] = mine[:, :quarter] + edge_in[1]

    @pl.when(jnp.logical_not(last))
    def _():
        edge(0).wait_recv()
        mine[:, mean - quarter :] = mine[:, mean - quarter :] + edge_in[0]

    each(own_copies(), start)

    @pl.when(jnp.logical_not(first))
    def _():
        def tail(head, _):
            absorb(head, edge_in[1, head], before_own(mean * rank, quarter))
            return 0

        lax.fori_loop(0, KV_HEADS, tail, 0)

    @pl.when(side == 1)
    def _():
        arrived(beside, beside_recv)

        def before(head, _):
            absorb(head, beside[head], before_own(mean * mate, mean))
            return 0

        lax.fori_loop(0, KV_HEADS, before, 0)

    for s in range(planes):
        with_near = s < plane
        with_far = row == 1 if s == 0 else s <= plane

        if s < planes - 1:

            @pl.when(with_near)
            def _(s=s):
                arrived(near[s].at[0], near_recv.at[s, 0])
                each(near_copies(s), start)

        @pl.when(with_far)
        def _(s=s):
            arrived(far[s].at[0], far_recv.at[s, 0])
            each(far_copies(s), start)

        if s < planes - 1:

            @pl.when(with_near)
            def _(s=s):
                arrived(near[s].at[1], near_recv.at[s, 1])
                absorb_pair(near[s], None)

        @pl.when(with_far)
        def _(s=s):
            arrived(far[s].at[1], far_recv.at[s, 1])
            follows = (side == 0) & (row == 1 - s)
            absorb_pair(far[s], follows if s < 2 else None)

    alive = lax.broadcasted_iota(jnp.int32, (slots, HEAD_DIM), 0) < own_count

    def write(head, _):
        result = (total[head] / weight_sum[head]).T
        for g in range(GROUP):
            column = pl.multiple_of((head * GROUP + g) * HEAD_DIM, HEAD_DIM)
            piece = jnp.where(alive, result[g * slots : (g + 1) * slots], 0.0)
            out_ref[:, pl.ds(column, HEAD_DIM)] = piece.astype(jnp.bfloat16)
        return 0

    lax.fori_loop(0, KV_HEADS, write, 0)

    @pl.when(jnp.logical_not(first))
    def _():
        edge(0).wait_send()

    @pl.when(jnp.logical_not(last))
    def _():
        edge(1).wait_send()

    each(own_copies(), finish)
    for s in range(planes):
        if s < planes - 1:

            @pl.when(s < plane)
            def _(s=s):
                each(near_copies(s), finish)

        @pl.when(row == 1 if s == 0 else s <= plane)
        def _(s=s):
            each(far_copies(s), finish)


def per_device(ranks, queries, patch_keys, patch_values, patch_counts):
    slots = patch_keys.shape[0]
    mean = slots * 2 // 3
    quarter = mean // 4
    lanes = GROUP * slots
    planes = ranks // 4
    return pl.pallas_call(
        functools.partial(kernel, ranks),
        out_shape=jax.ShapeDtypeStruct(queries.shape, jnp.bfloat16),
        in_specs=[pl.BlockSpec(memory_space=pltpu.VMEM)] * 3
        + [pl.BlockSpec(memory_space=pltpu.SMEM)],
        out_specs=pl.BlockSpec(memory_space=pltpu.VMEM),
        scratch_shapes=[
            [pltpu.VMEM((2, KV_HEADS, mean, 2 * HEAD_DIM), jnp.bfloat16)] * (planes - 1),
            [pltpu.VMEM((2, KV_HEADS, mean, 2 * HEAD_DIM), jnp.bfloat16)] * planes,
            pltpu.VMEM((KV_HEADS, mean, 2 * HEAD_DIM), jnp.bfloat16),
            pltpu.VMEM((KV_HEADS, mean, 2 * HEAD_DIM), jnp.bfloat16),
            pltpu.VMEM((2, KV_HEADS, quarter, 2 * HEAD_DIM), jnp.bfloat16),
            pltpu.VMEM((2, KV_HEADS, quarter, 2 * HEAD_DIM), jnp.bfloat16),
            pltpu.VMEM((KV_HEADS, lanes, HEAD_DIM), jnp.bfloat16),
            pltpu.VMEM((KV_HEADS, HEAD_DIM, lanes), jnp.float32),
            pltpu.VMEM((KV_HEADS, 1, lanes), jnp.float32),
            pltpu.VMEM((KV_HEADS, 1, lanes), jnp.float32),
            pltpu.SemaphoreType.DMA((3,)),
            pltpu.SemaphoreType.DMA((planes, 3)),
            pltpu.SemaphoreType.DMA((planes,)),
            pltpu.SemaphoreType.DMA,
            pltpu.SemaphoreType.DMA((planes, 2)),
            pltpu.SemaphoreType.DMA((planes, 2)),
            pltpu.SemaphoreType.DMA((2,)),
            pltpu.SemaphoreType.DMA((2,)),
        ],
        compiler_params=pltpu.CompilerParams(
            collective_id=0, has_side_effects=True, vmem_limit_bytes=52 * 2**20
        ),
    )(queries, patch_keys, patch_values, patch_counts)


def solution(mesh):
    placed = (
        P(("groups", "ctx"), None),
        P(("groups", "ctx"), None),
        P(("groups", "ctx"), None),
        P("groups"),
    )
    return jax.shard_map(
        functools.partial(per_device, mesh.shape["ctx"]),
        mesh=mesh,
        in_specs=placed,
        out_specs=P(("groups", "ctx"), None),
        check_vma=False,
    )
```

time: 182 us -> 43.7 us (0.24)
  waiting for transfers between devices: 75.5 us -> 0 us
  Pallas kernels: 0 us -> 39 us
  matrix products: 33.3 us -> 0 us
  local copies, waits for them, and re-layouts: 31.1 us -> 4.52 us
  other arithmetic: 23.1 us -> 0 us
  between operations: 13.5 us -> 0.01 us
  loops' own time: 4.08 us -> 0 us
    all_gather x2 -> x0, waiting for transfers between devices: 74.1 us -> none  [the longest x1 37.6 us: per_device(): lax.all_gather(patch_keys, 'ctx', axis=0, tiled=True)]
    pallas_call x0 -> x1, Pallas kernels: none -> 39 us  [per_device(): pl.pallas_call(functools.partial(kernel, ranks), out_shape=jax.ShapeDtype...]
    dot_general x12 -> x0, matrix products: 33.3 us -> none  [the longest x6 19.9 us: compute(): jnp.einsum('kgrm,mkd->kgrd', rounded, value_block, preferred_element_type...]
    reshape x4 -> x0, local copies, waits for them, and re-layouts: 14 us -> none  [the longest x1 5.56 us: attend(): value_blocks = value_rows.reshape(pieces, block_len, KV_HEADS, HEAD_DIM)]
    reduce_sum x6 -> x0, other arithmetic: 11.7 us -> none  [compute(): weight_sum = weight_sum * rescale + jnp.sum(weights, axis=-1)]
    dynamic_slice x20 -> x0, local copies, waits for them, and re-layouts: 5.67 us -> none  [the longest x18 3.79 us: attend(): lax.scan(accumulate, initial, (key_blocks, value_blocks, place_blocks, li...]
    add x19 -> x0, other arithmetic: 4.37 us -> none  [the longest x6 3.79 us: per_device(): own_place = own_start + slot_order]
    unnamed x5 -> x9, local copies, waits for them, and re-layouts: 8.71 us -> 4.52 us
  transfers between devices with their start and end apart: 2 -> 0, of which waited for: 2 -> 0; matrix products, arithmetic and copies ran while one was open for 11% -> 0% of each run, Pallas kernels for 0% -> 0%
where the time goes in v1:
time: 43.7 us; the launch traced here: 43.5 us
  Pallas kernels  39 us (89%)
  local copies, waits for them, and re-layouts  4.52 us (10%)
    pallas_call x1, Pallas kernels, per_device(): pl.pallas_call(functools.partial(kernel, ranks), out_shape=jax.ShapeDtype...  39 us
    unnamed x9, local copies, waits for them, and re-layouts  4.52 us

profile of v1, /device:TPU:25, one launch (start us, length us, event | category | flops | bytes accessed | tf_op | source)
XLA Modules:
  0.0 43.5 jit_solution(8437437398096484483)
XLA Ops:
  0.0 0.0 copy-start
  0.0 1.1 %copy-done = bf16[192,2048]{1,0:T(8,128)(2,1)S(1)} copy-done((bf16[192,2048]{1,0:T(8,128)(2,1)S(1)}, bf16[192,2048]{1,0:T(8,128)(2,1)}, u32[]{:S(2)}) %copy-start) | copy-done | bytes 786456
  1.1 0.0 copy-start.1
  1.1 0.9 %copy-done.1 = bf16[192,512]{1,0:T(8,128)(2,1)S(1)} copy-done((bf16[192,512]{1,0:T(8,128)(2,1)S(1)}, bf16[192,512]{1,0:T(8,128)(2,1)}, u32[]{:S(2)}) %copy-start.1) | copy-done | bytes 196632
  2.1 0.0 copy-start.2
  2.1 0.9 %copy-done.2 = bf16[192,512]{1,0:T(8,128)(2,1)S(1)} copy-done((bf16[192,512]{1,0:T(8,128)(2,1)S(1)}, bf16[192,512]{1,0:T(8,128)(2,1)}, u32[]{:S(2)}) %copy-start.2) | copy-done | bytes 196632
  3.0 0.0 copy-start.3
  3.0 0.7 %copy-done.3 = s32[16]{0:T(128)S(1)} copy-done((s32[16]{0:T(128)S(1)}, s32[16]{0:T(128)}, u32[]{:S(2)}) %copy-start.3) | copy-done | bytes 88
  3.6 39.0 %shard_map.46 = bf16[192,2048]{1,0:T(8,128)(2,1)S(1)} custom-call(bf16[192,2048]{1,0:T(8,128)(2,1)S(1)} %copy-done, bf16[192,512]{1,0:T(8,128)(2,1)S(1)} %copy-done.1, bf16[192,512]{1,0:T(8,128)(2,1)S(1)} %copy-done.2, s32[16]{0:T(128)S(1)} %copy-done.3), custom_call_target="tpu_custom_call" | custom-call | tf_op jit(solution)/shard_map/pallas_call | solution.py:342
  42.6 0.9 %copy.6 = bf16[192,2048]{1,0:T(8,128)(2,1)} copy(bf16[192,2048]{1,0:T(8,128)(2,1)S(1)} %shard_map.46) | data formatting | bytes 1572864
Async XLA Ops:
  0.0 1.1 %copy-start = (bf16[192,2048]{1,0:T(8,128)(2,1)S(1)}, bf16[192,2048]{1,0:T(8,128)(2,1)}, u32[]{:S(2)}) copy-start(bf16[192,2048]{1,0:T(8,128)(2,1)} %q_ref.1) | copy-start | bytes 2359300
  1.1 0.9 %copy-start.1 = (bf16[192,512]{1,0:T(8,128)(2,1)S(1)}, bf16[192,512]{1,0:T(8,128)(2,1)}, u32[]{:S(2)}) copy-start(bf16[192,512]{1,0:T(8,128)(2,1)} %k_ref.1) | copy-start | bytes 589828
  2.1 0.9 %copy-start.2 = (bf16[192,512]{1,0:T(8,128)(2,1)S(1)}, bf16[192,512]{1,0:T(8,128)(2,1)}, u32[]{:S(2)}) copy-start(bf16[192,512]{1,0:T(8,128)(2,1)} %v_ref.1) | copy-start | bytes 589828
  3.0 0.7 %copy-start.3 = (s32[16]{0:T(128)S(1)}, s32[16]{0:T(128)}, u32[]{:S(2)}) copy-start(s32[16]{0:T(128)} %counts_ref.1) | copy-start | bytes 196

commit v2 on v1

v2 whole, which is shorter than its diff:
```python
import functools

import jax
import jax.numpy as jnp
from jax import lax
from jax.experimental import pallas as pl
from jax.experimental.pallas import tpu as pltpu
from jax.sharding import PartitionSpec as P

KV_HEADS = 4
GROUP = 4
HEAD_DIM = 128
HIDDEN = -1e30
LOG2E = 1.4426950408889634
EXPONENT_SCALE = LOG2E * HEAD_DIM ** (-0.5)
MESH = pl.DeviceIdType.MESH

FAR_PLACE = 2**20


def kernel(
    ranks,
    q_hbm,
    k_hbm,
    v_hbm,
    counts_ref,
    out_ref,
    k_ref,
    v_ref,
    near,
    far,
    beside,
    mine,
    edge_out,
    edge_in,
    stacked,
    total,
    highest,
    weight_sum,
    load_sems,
    query_sems,
    own_send,
    near_send,
    far_send,
    beside_recv,
    near_recv,
    far_recv,
    edge_send,
    edge_recv,
):
    slots = k_ref.shape[0]
    quarter = edge_in.shape[2]
    mean = 4 * quarter
    planes = ranks // 4
    lanes = GROUP * slots
    part_index = lax.axis_index("groups")
    rank = lax.axis_index("ctx")
    plane, row, side = rank // 4, (rank // 2) % 2, rank % 2
    mate = rank + 1 - 2 * side
    over = rank + 2 - 4 * row
    first, last = rank == 0, rank == ranks - 1

    partners = (
        (mate, None),
        (over, None),
        (rank - 1, (side == 0) & (rank > 0)),
        (rank + 1, (side == 1) & (rank < ranks - 1)),
        (rank - 4, plane > 0),
        (rank + 4, plane < planes - 1),
    )
    barrier = pltpu.get_barrier_semaphore()
    expected = 0
    for partner, there in partners:
        if there is None:
            pl.semaphore_signal(
                barrier, inc=1, device_id=(part_index, partner), device_id_type=MESH
            )
            expected = expected + 1
        else:

            @pl.when(there)
            def _(partner=partner):
                pl.semaphore_signal(
                    barrier, inc=1, device_id=(part_index, partner), device_id_type=MESH
                )

            expected = expected + there.astype(jnp.int32)

    loads = (
        pltpu.make_async_copy(k_hbm, k_ref, load_sems.at[0]),
        pltpu.make_async_copy(v_hbm, v_ref, load_sems.at[1]),
    )
    for load in loads:
        load.start()
    query_loads = [
        pltpu.make_async_copy(
            q_hbm.at[:, pl.ds((head * GROUP + g) * HEAD_DIM, HEAD_DIM)],
            stacked.at[head, pl.ds(g * slots, slots)],
            query_sems.at[head * GROUP + g],
        )
        for head in range(KV_HEADS)
        for g in range(GROUP)
    ]
    for load in query_loads:
        load.start()

    own_start = lax.fori_loop(
        0, ranks, lambda j, s: s + jnp.where(j < rank, counts_ref[j], 0), jnp.int32(0)
    )
    own_count = counts_ref[rank]

    place = lax.broadcasted_iota(jnp.int32, (slots, slots), 0) + (mean * rank - quarter - own_start)
    slot = lax.broadcasted_iota(jnp.int32, (slots, slots), 1)
    pick = jnp.where((place == slot) & (slot < own_count), 1.0, 0.0).astype(jnp.bfloat16)
    for part, ref in enumerate((k_ref, v_ref)):
        loads[part].wait()
        placed = jnp.dot(pick, ref[...], preferred_element_type=jnp.float32).astype(jnp.bfloat16)
        half = slice(part * HEAD_DIM, (part + 1) * HEAD_DIM)
        for head in range(KV_HEADS):
            rows = placed[:, head * HEAD_DIM : (head + 1) * HEAD_DIM]
            edge_out[0, head, :, half] = rows[:quarter]
            mine[1, head, :quarter, half] = rows[quarter : 2 * quarter]
            mine[0, head, :, half] = rows[2 * quarter : 4 * quarter]
            mine[1, head, quarter:, half] = rows[4 * quarter : 5 * quarter]
            edge_out[1, head, :, half] = rows[5 * quarter :]

    @pl.when(first)
    def _():
        edge_in[1] = jnp.zeros(edge_in.shape[1:], edge_in.dtype)

    pl.semaphore_wait(barrier, expected)

    def copy(source, landing, send_sem, recv_sem, target):
        return pltpu.make_async_remote_copy(
            src_ref=source,
            dst_ref=landing,
            send_sem=send_sem,
            recv_sem=recv_sem,
            device_id=(part_index, target),
            device_id_type=MESH,
        )

    def edge(which):
        return copy(
            edge_out.at[which],
            edge_in.at[which],
            edge_send.at[which],
            edge_recv.at[which],
            (rank + 2 * which - 1 + ranks) % ranks,
        )

    more = plane < planes - 1

    def own_copies(p):
        source = mine.at[p]
        along = (None, None)
        if planes > 1:
            along = (
                more,
                copy(source, near[0].at[0, p], own_send.at[p, 0], near_recv.at[0, 0, p], rank + 4),
            )
        return (
            (row == 0, copy(source, far[0].at[0, p], own_send.at[p, 1], far_recv.at[0, 0, p], over)),
            along,
            (side == 0, copy(source, beside.at[p], own_send.at[p, 2], beside_recv.at[p], mate)),
        )

    def near_copies(s, p):
        source = near[s].at[0, p]
        along = (None, None)
        if s + 1 < planes - 1:
            along = (
                more,
                copy(
                    source,
                    near[s + 1].at[0, p],
                    near_send.at[s, p, 0],
                    near_recv.at[s + 1, 0, p],
                    rank + 4,
                ),
            )
        return (
            along,
            (
                True,
                copy(
                    source,
                    far[s + 1].at[0, p],
                    near_send.at[s, p, 1],
                    far_recv.at[s + 1, 0, p],
                    over,
                ),
            ),
            (
                True,
                copy(source, near[s].at[1, p], near_send.at[s, p, 2], near_recv.at[s, 1, p], mate),
            ),
        )

    def far_copies(s, p):
        return (
            (
                True,
                copy(far[s].at[0, p], far[s].at[1, p], far_send.at[s, p], far_recv.at[s, 1, p], mate),
            ),
        )

    def each(copies, act):
        for wanted, item in copies:
            if wanted is True:
                act(item)
            elif wanted is not None:

                @pl.when(wanted)
                def _(item=item):
                    act(item)

    def start(item):
        item.start()

    def finish(item):
        item.wait_send()

    def arrived(landing, recv_sem):
        copy(landing, landing, own_send.at[0, 0], recv_sem, mate).wait_recv()

    @pl.when(jnp.logical_not(first))
    def _():
        edge(0).start()

    @pl.when(jnp.logical_not(last))
    def _():
        edge(1).start()

    each(own_copies(0), start)

    for load in query_loads:
        load.wait()

    @pl.when(jnp.logical_not(first))
    def _():
        edge(1).wait_recv()
        mine[1, :, :quarter] = mine[1, :, :quarter] + edge_in[1]

    @pl.when(jnp.logical_not(last))
    def _():
        edge(0).wait_recv()
        mine[1, :, quarter:] = mine[1, :, quarter:] + edge_in[0]

    each(own_copies(1), start)

    def each_head(act):
        if planes <= 4:
            for head in range(KV_HEADS):
                act(head)
        else:

            def one(head, _):
                act(head)
                return 0

            lax.fori_loop(0, KV_HEADS, one, 0)

    def scores_of(keys, head):
        return lax.dot_general(
            keys, stacked[head], (((1,), (1,)), ((), ())), preferred_element_type=jnp.float32
        )

    def blend(values, weights):
        return lax.dot_general(
            values,
            weights.astype(jnp.bfloat16),
            (((0,), (0,)), ((), ())),
            preferred_element_type=jnp.float32,
        )

    def head_columns(head):
        return pl.ds(pl.multiple_of(head * HEAD_DIM, HEAD_DIM), HEAD_DIM)

    def before_own(first_place):
        at = lax.broadcasted_iota(jnp.int32, (quarter, lanes), 0) + first_place
        return at < own_start

    def own(head):
        tail = edge_in[1, head]
        keys = jnp.concatenate([k_ref[:, head_columns(head)], tail[:, :HEAD_DIM]])
        values = jnp.concatenate([v_ref[:, head_columns(head)], tail[:, HEAD_DIM:]])
        scores = scores_of(keys, head)
        key_slot = lax.broadcasted_iota(jnp.int32, (slots, lanes), 0)
        query_slot = lax.broadcasted_iota(jnp.int32, (slots, lanes), 1) % slots
        scores = jnp.concatenate(
            [
                jnp.where(key_slot <= query_slot, scores[:slots], HIDDEN),
                jnp.where(before_own(mean * rank), scores[slots:], HIDDEN),
            ]
        )
        top = jnp.max(scores, axis=0, keepdims=True)
        weights = jnp.exp2((scores - top) * EXPONENT_SCALE)
        highest[head] = top
        weight_sum[head] = jnp.sum(weights, axis=0, keepdims=True)
        total[head] = blend(values, weights)

    def absorb(head, rows, visible):
        scores = scores_of(rows[:, :HEAD_DIM], head)
        if visible is not None:
            scores = jnp.concatenate(
                [scores[:-quarter], jnp.where(visible, scores[-quarter:], HIDDEN)]
            )
        before = highest[head]
        top = jnp.maximum(before, jnp.max(scores, axis=0, keepdims=True))
        rescale = jnp.exp2((before - top) * EXPONENT_SCALE)
        weights = jnp.exp2((scores - top) * EXPONENT_SCALE)
        highest[head] = top
        weight_sum[head] = weight_sum[head] * rescale + jnp.sum(weights, axis=0, keepdims=True)
        total[head] = total[head] * rescale + blend(rows[:, HEAD_DIM:], weights)

    def absorb_pair(pair, follows):
        visible = None
        if follows is not None:
            visible = before_own(jnp.where(follows, mean * rank - quarter, -FAR_PLACE))

        def one(head):
            rows = jnp.concatenate([pair[i, p, head] for i in (0, 1) for p in (0, 1)])
            absorb(head, rows, visible)

        each_head(one)

    each_head(own)

    @pl.when(side == 1)
    def _():
        for p in (0, 1):
            arrived(beside.at[p], beside_recv.at[p])
        visible = before_own(mean * rank - quarter)

        def one(head):
            absorb(head, jnp.concatenate([beside[p, head] for p in (0, 1)]), visible)

        each_head(one)

    for s in range(planes):
        with_near = s < plane
        with_far = row == 1 if s == 0 else s <= plane

        for p in (0, 1):
            if s < planes - 1:

                @pl.when(with_near)
                def _(s=s, p=p):
                    arrived(near[s].at[0, p], near_recv.at[s, 0, p])
                    each(near_copies(s, p), start)

            @pl.when(with_far)
            def _(s=s, p=p):
                arrived(far[s].at[0, p], far_recv.at[s, 0, p])
                each(far_copies(s, p), start)

        if s < planes - 1:

            @pl.when(with_near)
            def _(s=s):
                for p in (0, 1):
                    arrived(near[s].at[1, p], near_recv.at[s, 1, p])
                absorb_pair(near[s], None)

        @pl.when(with_far)
        def _(s=s):
            for p in (0, 1):
                arrived(far[s].at[1, p], far_recv.at[s, 1, p])
            absorb_pair(far[s], (side == 0) & (row == 1 - s) if s < 2 else None)

    alive = lax.broadcasted_iota(jnp.int32, (slots, HEAD_DIM), 0) < own_count

    def write(head):
        result = (total[head] / weight_sum[head]).T
        for g in range(GROUP):
            column = pl.multiple_of((head * GROUP + g) * HEAD_DIM, HEAD_DIM)
            piece = jnp.where(alive, result[g * slots : (g + 1) * slots], 0.0)
            out_ref[:, pl.ds(column, HEAD_DIM)] = piece.astype(jnp.bfloat16)

    each_head(write)

    @pl.when(jnp.logical_not(first))
    def _():
        edge(0).wait_send()

    @pl.when(jnp.logical_not(last))
    def _():
        edge(1).wait_send()

    for p in (0, 1):
        each(own_copies(p), finish)
        for s in range(planes):
            if s < planes - 1:

                @pl.when(s < plane)
                def _(s=s, p=p):
                    each(near_copies(s, p), finish)

            @pl.when(row == 1 if s == 0 else s <= plane)
            def _(s=s, p=p):
                each(far_copies(s, p), finish)


def per_device(ranks, queries, patch_keys, patch_values, patch_counts):
    slots, width = patch_keys.shape
    quarter = slots // 6
    lanes = GROUP * slots
    planes = ranks // 4
    two_parts = (2, KV_HEADS, 2 * quarter, 2 * HEAD_DIM)
    pair = pltpu.VMEM((2, *two_parts), jnp.bfloat16)
    edges = pltpu.VMEM((2, KV_HEADS, quarter, 2 * HEAD_DIM), jnp.bfloat16)
    return pl.pallas_call(
        functools.partial(kernel, ranks),
        out_shape=jax.ShapeDtypeStruct(queries.shape, jnp.bfloat16),
        in_specs=[pl.BlockSpec(memory_space=pl.ANY)] * 3
        + [pl.BlockSpec(memory_space=pltpu.SMEM)],
        out_specs=pl.BlockSpec(memory_space=pltpu.VMEM),
        scratch_shapes=[
            pltpu.VMEM((slots, width), jnp.bfloat16),
            pltpu.VMEM((slots, width), jnp.bfloat16),
            [pair] * (planes - 1),
            [pair] * planes,
            pltpu.VMEM(two_parts, jnp.bfloat16),
            pltpu.VMEM(two_parts, jnp.bfloat16),
            edges,
            edges,
            pltpu.VMEM((KV_HEADS, lanes, HEAD_DIM), jnp.bfloat16),
            pltpu.VMEM((KV_HEADS, HEAD_DIM, lanes), jnp.float32),
            pltpu.VMEM((KV_HEADS, 1, lanes), jnp.float32),
            pltpu.VMEM((KV_HEADS, 1, lanes), jnp.float32),
            pltpu.SemaphoreType.DMA((2,)),
            pltpu.SemaphoreType.DMA((KV_HEADS * GROUP,)),
            pltpu.SemaphoreType.DMA((2, 3)),
            pltpu.SemaphoreType.DMA((planes, 2, 3)),
            pltpu.SemaphoreType.DMA((planes, 2)),
            pltpu.SemaphoreType.DMA((2,)),
            pltpu.SemaphoreType.DMA((planes, 2, 2)),
            pltpu.SemaphoreType.DMA((planes, 2, 2)),
            pltpu.SemaphoreType.DMA((2,)),
            pltpu.SemaphoreType.DMA((2,)),
        ],
        compiler_params=pltpu.CompilerParams(
            collective_id=0, has_side_effects=True, vmem_limit_bytes=60 * 2**20
        ),
    )(queries, patch_keys, patch_values, patch_counts)


def solution(mesh):
    placed = (
        P(("groups", "ctx"), None),
        P(("groups", "ctx"), None),
        P(("groups", "ctx"), None),
        P("groups"),
    )
    return jax.shard_map(
        functools.partial(per_device, mesh.shape["ctx"]),
        mesh=mesh,
        in_specs=placed,
        out_specs=P(("groups", "ctx"), None),
        check_vma=False,
    )
```

time: 43.7 us -> 37.3 us (0.85)
  Pallas kernels: 39 us -> 35 us
  local copies, waits for them, and re-layouts: 4.52 us -> 2.09 us
    pallas_call x1, Pallas kernels: 39 us -> 35 us  [per_device(): pl.pallas_call(functools.partial(kernel, ranks), out_shape=jax.ShapeDtype...]
    unnamed x9 -> x1, local copies, waits for them, and re-layouts: 4.52 us -> 2.09 us
where the time goes in v2:
time: 37.3 us; the launch traced here: 37.1 us
  Pallas kernels  35 us (94%)
  local copies, waits for them, and re-layouts  2.09 us (6%)
    pallas_call x1, Pallas kernels, per_device(): pl.pallas_call(functools.partial(kernel, ranks), out_shape=jax.ShapeDtype...  35 us
    unnamed x1, local copies, waits for them, and re-layouts  2.09 us

profile of v2, /device:TPU:25, one launch (start us, length us, event | category | flops | bytes accessed | tf_op | source)
XLA Modules:
  0.0 37.1 jit_solution(14949473243550451695)
XLA Ops:
  0.0 35.0 %shard_map.46 = bf16[192,2048]{1,0:T(8,128)(2,1)} custom-call(bf16[192,2048]{1,0:T(8,128)(2,1)} %q_hbm.1, bf16[192,512]{1,0:T(8,128)(2,1)} %k_hbm.1, bf16[192,512]{1,0:T(8,128)(2,1)} %v_hbm.1, s32[16]{0:T(128)} %counts_ref.1), custom_call_target="tpu_custom_call" | custom-call | tf_op jit(solution)/shard_map/pallas_call | solution.py:413
  35.0 2.1 %copy.6 = bf16[192,2048]{1,0:T(8,128)(2,1)} copy(bf16[192,2048]{1,0:T(8,128)(2,1)} %shard_map.46) | data formatting | bytes 1572864

commit v3 on v2

--- a/solution.py
+++ b/solution.py
@@ -23,8 +23,9 @@
     q_hbm,
     k_hbm,
     v_hbm,
+    counts_hbm,
+    out_ref,
     counts_ref,
-    out_ref,
     k_ref,
     v_ref,
     near,
@@ -34,6 +35,7 @@
     edge_out,
     edge_in,
     stacked,
+    turned,
     total,
     highest,
     weight_sum,
@@ -89,6 +91,7 @@
     loads = (
         pltpu.make_async_copy(k_hbm, k_ref, load_sems.at[0]),
         pltpu.make_async_copy(v_hbm, v_ref, load_sems.at[1]),
+        pltpu.make_async_copy(counts_hbm, counts_ref, load_sems.at[2]),
     )
     for load in loads:
         load.start()
@@ -104,6 +107,7 @@
     for load in query_loads:
         load.start()
 
+    loads[2].wait()
     own_start = lax.fori_loop(
         0, ranks, lambda j, s: s + jnp.where(j < rank, counts_ref[j], 0), jnp.int32(0)
     )
@@ -198,11 +202,9 @@
         )
 
     def far_copies(s, p):
+        source = far[s].at[0, p]
         return (
-            (
-                True,
-                copy(far[s].at[0, p], far[s].at[1, p], far_send.at[s, p], far_recv.at[s, 1, p], mate),
-            ),
+            (True, copy(source, far[s].at[1, p], far_send.at[s, p], far_recv.at[s, 1, p], mate)),
         )
 
     def each(copies, act):
@@ -236,6 +238,8 @@
 
     for load in query_loads:
         load.wait()
+    for head in range(KV_HEADS):
+        turned[head] = stacked[head].T
 
     @pl.when(jnp.logical_not(first))
     def _():
@@ -263,7 +267,7 @@
 
     def scores_of(keys, head):
         return lax.dot_general(
-            keys, stacked[head], (((1,), (1,)), ((), ())), preferred_element_type=jnp.float32
+            keys, turned[head], (((1,), (0,)), ((), ())), preferred_element_type=jnp.float32
         )
 
     def blend(values, weights):
@@ -300,52 +304,71 @@
         weight_sum[head] = jnp.sum(weights, axis=0, keepdims=True)
         total[head] = blend(values, weights)
 
-    def absorb(head, rows, visible):
-        scores = scores_of(rows[:, :HEAD_DIM], head)
-        if visible is not None:
-            scores = jnp.concatenate(
-                [scores[:-quarter], jnp.where(visible, scores[-quarter:], HIDDEN)]
-            )
-        before = highest[head]
-        top = jnp.maximum(before, jnp.max(scores, axis=0, keepdims=True))
-        rescale = jnp.exp2((before - top) * EXPONENT_SCALE)
-        weights = jnp.exp2((scores - top) * EXPONENT_SCALE)
-        highest[head] = top
-        weight_sum[head] = weight_sum[head] * rescale + jnp.sum(weights, axis=0, keepdims=True)
-        total[head] = total[head] * rescale + blend(rows[:, HEAD_DIM:], weights)
+    def absorb_all(rows_of, visible):
+        def score(head):
+            rows = rows_of(head)
+            scores = scores_of(rows[:, :HEAD_DIM], head)
+            if visible is not None:
+                scores = jnp.concatenate(
+                    [scores[:-quarter], jnp.where(visible, scores[-quarter:], HIDDEN)]
+                )
+            return scores, rows[:, HEAD_DIM:]
+
+        def weigh(head, scores):
+            before = highest[head]
+            top = jnp.maximum(before, jnp.max(scores, axis=0, keepdims=True))
+            rescale = jnp.exp2((before - top) * EXPONENT_SCALE)
+            weights = jnp.exp2((scores - top) * EXPONENT_SCALE)
+            highest[head] = top
+            weight_sum[head] = weight_sum[head] * rescale + jnp.sum(weights, axis=0, keepdims=True)
+            return rescale, weights.astype(jnp.bfloat16)
+
+        def gather(head, rescale, weights, values):
+            total[head] = total[head] * rescale + blend(values, weights)
+
+        if planes > 4:
+
+            def one(head, _):
+                scores, values = score(head)
+                gather(head, *weigh(head, scores), values)
+                return 0
+
+            lax.fori_loop(0, KV_HEADS, one, 0)
+            return
+        held = [score(head) for head in range(KV_HEADS)]
+        weighed = [weigh(head, held[head][0]) for head in range(KV_HEADS)]
+        for head in range(KV_HEADS):
+            gather(head, *weighed[head], held[head][1])
 
     def absorb_pair(pair, follows):
         visible = None
         if follows is not None:
             visible = before_own(jnp.where(follows, mean * rank - quarter, -FAR_PLACE))
 
-        def one(head):
-            rows = jnp.concatenate([pair[i, p, head] for i in (0, 1) for p in (0, 1)])
-            absorb(head, rows, visible)
-
-        each_head(one)
-
-    each_head(own)
-
-    @pl.when(side == 1)
-    def _():
-        for p in (0, 1):
-            arrived(beside.at[p], beside_recv.at[p])
-        visible = before_own(mean * rank - quarter)
-
-        def one(head):
-            absorb(head, jnp.concatenate([beside[p, head] for p in (0, 1)]), visible)
-
-        each_head(one)
+        absorb_all(
+            lambda head: jnp.concatenate([pair[i, p, head] for i in (0, 1) for p in (0, 1)]), visible
+        )
+
+    def near_step(s):
+        @pl.when(s < plane)
+        def _():
+            for p in (0, 1):
+                arrived(near[s].at[1, p], near_recv.at[s, 1, p])
+            absorb_pair(near[s], None)
+
+    def far_step(s, when):
+        @pl.when(when)
+        def _():
+            for p in (0, 1):
+                arrived(far[s].at[1, p], far_recv.at[s, 1, p])
+            absorb_pair(far[s], (side == 0) & (row == 1 - s) if s < 2 else None)
 
     for s in range(planes):
-        with_near = s < plane
         with_far = row == 1 if s == 0 else s <= plane
-
         for p in (0, 1):
             if s < planes - 1:
 
-                @pl.when(with_near)
+                @pl.when(s < plane)
                 def _(s=s, p=p):
                     arrived(near[s].at[0, p], near_recv.at[s, 0, p])
                     each(near_copies(s, p), start)
@@ -355,19 +378,21 @@
                 arrived(far[s].at[0, p], far_recv.at[s, 0, p])
                 each(far_copies(s, p), start)
 
-        if s < planes - 1:
-
-            @pl.when(with_near)
-            def _(s=s):
+            if p == 0 and s == 0:
+                each_head(own)
+            elif p == 0:
+                near_step(s - 1)
+                far_step(s - 1, (s <= plane) & ((row == 1) if s == 1 else True))
+        if s == 0:
+
+            @pl.when(side == 1)
+            def _():
                 for p in (0, 1):
-                    arrived(near[s].at[1, p], near_recv.at[s, 1, p])
-                absorb_pair(near[s], None)
-
-        @pl.when(with_far)
-        def _(s=s):
-            for p in (0, 1):
-                arrived(far[s].at[1, p], far_recv.at[s, 1, p])
-            absorb_pair(far[s], (side == 0) & (row == 1 - s) if s < 2 else None)
+                    arrived(beside.at[p], beside_recv.at[p])
+                visible = before_own(mean * rank - quarter)
+                absorb_all(lambda head: jnp.concatenate([beside[p, head] for p in (0, 1)]), visible)
+
+        far_step(s, (s == plane) & ((row == 1) if s == 0 else True))
 
     alive = lax.broadcasted_iota(jnp.int32, (slots, HEAD_DIM), 0) < own_count
 
@@ -413,10 +438,10 @@
     return pl.pallas_call(
         functools.partial(kernel, ranks),
         out_shape=jax.ShapeDtypeStruct(queries.shape, jnp.bfloat16),
-        in_specs=[pl.BlockSpec(memory_space=pl.ANY)] * 3
-        + [pl.BlockSpec(memory_space=pltpu.SMEM)],
+        in_specs=[pl.BlockSpec(memory_space=pl.ANY)] * 4,
         out_specs=pl.BlockSpec(memory_space=pltpu.VMEM),
         scratch_shapes=[
+            pltpu.SMEM(patch_counts.shape, jnp.int32),
             pltpu.VMEM((slots, width), jnp.bfloat16),
             pltpu.VMEM((slots, width), jnp.bfloat16),
             [pair] * (planes - 1),
@@ -426,10 +451,11 @@
             edges,
             edges,
             pltpu.VMEM((KV_HEADS, lanes, HEAD_DIM), jnp.bfloat16),
+            pltpu.VMEM((KV_HEADS, HEAD_DIM, lanes), jnp.bfloat16),
             pltpu.VMEM((KV_HEADS, HEAD_DIM, lanes), jnp.float32),
             pltpu.VMEM((KV_HEADS, 1, lanes), jnp.float32),
             pltpu.VMEM((KV_HEADS, 1, lanes), jnp.float32),
-            pltpu.SemaphoreType.DMA((2,)),
+            pltpu.SemaphoreType.DMA((3,)),
             pltpu.SemaphoreType.DMA((KV_HEADS * GROUP,)),
             pltpu.SemaphoreType.DMA((2, 3)),
             pltpu.SemaphoreType.DMA((planes, 2, 3)),

time: 37.3 us -> 33.9 us (0.909)
  Pallas kernels: 35 us -> 31.6 us
    pallas_call x1, Pallas kernels: 35 us -> 31.6 us  [per_device(): pl.pallas_call(functools.partial(kernel, ranks), out_shape=jax.ShapeDtype...]
where the time goes in v3:
time: 33.9 us; the launch traced here: 33.7 us
  Pallas kernels  31.6 us (93%)
  local copies, waits for them, and re-layouts  2.09 us (6%)
    pallas_call x1, Pallas kernels, per_device(): pl.pallas_call(functools.partial(kernel, ranks), out_shape=jax.ShapeDtype...  31.6 us
    unnamed x1, local copies, waits for them, and re-layouts  2.09 us

profile of v3, /device:TPU:25, one launch (start us, length us, event | category | flops | bytes accessed | tf_op | source)
XLA Modules:
  0.0 33.7 jit_solution(16407633979079776249)
XLA Ops:
  0.0 31.6 %shard_map.46 = bf16[192,2048]{1,0:T(8,128)(2,1)} custom-call(bf16[192,2048]{1,0:T(8,128)(2,1)} %q_hbm.1, bf16[192,512]{1,0:T(8,128)(2,1)} %k_hbm.1, bf16[192,512]{1,0:T(8,128)(2,1)} %v_hbm.1, s32[16]{0:T(128)} %counts_hbm.1), custom_call_target="tpu_custom_call" | custom-call | tf_op jit(solution)/shard_map/pallas_call | solution.py:438
  31.6 2.1 %copy.6 = bf16[192,2048]{1,0:T(8,128)(2,1)} copy(bf16[192,2048]{1,0:T(8,128)(2,1)} %shard_map.46) | data formatting | bytes 1572864

commit v4 on v3

--- a/solution.py
+++ b/solution.py
@@ -378,10 +378,12 @@
                 arrived(far[s].at[0, p], far_recv.at[s, 0, p])
                 each(far_copies(s, p), start)
 
-            if p == 0 and s == 0:
-                each_head(own)
+            if s == 0:
+                if p == 0:
+                    each_head(own)
             elif p == 0:
                 near_step(s - 1)
+            else:
                 far_step(s - 1, (s <= plane) & ((row == 1) if s == 1 else True))
         if s == 0:
 

time: 33.9 us -> 33.6 us (level)
  no operation moved by 1% of the time
where the time goes in v4:
time: 33.6 us; the launch traced here: 33.4 us
  Pallas kernels  31.3 us (93%)
  local copies, waits for them, and re-layouts  2.09 us (6%)
    pallas_call x1, Pallas kernels, per_device(): pl.pallas_call(functools.partial(kernel, ranks), out_shape=jax.ShapeDtype...  31.3 us
    unnamed x1, local copies, waits for them, and re-layouts  2.09 us

profile of v4, /device:TPU:25, one launch (start us, length us, event | category | flops | bytes accessed | tf_op | source)
XLA Modules:
  0.0 33.4 jit_solution(2252900854033827249)
XLA Ops:
  0.0 31.3 %shard_map.46 = bf16[192,2048]{1,0:T(8,128)(2,1)} custom-call(bf16[192,2048]{1,0:T(8,128)(2,1)} %q_hbm.1, bf16[192,512]{1,0:T(8,128)(2,1)} %k_hbm.1, bf16[192,512]{1,0:T(8,128)(2,1)} %v_hbm.1, s32[16]{0:T(128)} %counts_hbm.1), custom_call_target="tpu_custom_call" | custom-call | tf_op jit(solution)/shard_map/pallas_call | solution.py:440
  31.3 2.1 %copy.6 = bf16[192,2048]{1,0:T(8,128)(2,1)} copy(bf16[192,2048]{1,0:T(8,128)(2,1)} %shard_map.46) | data formatting | bytes 1572864
